TPU v7x, 512 devices: a whole 4x4x16 slice. The times are simulated.
512 devices in a mesh: row: 8 (over x_lo, y), col: 16 (over z), vc: 4 (over x_hi, core).
Axes of the slice: x: 4 (x_hi: 2, x_lo: 2; x = x_hi * 2 + x_lo), y: 4, z: 16, core: 2. Of those that a mesh axis runs over, the one named last changes fastest.
Arguments:
- amplitudes: bfloat16 [32, 32, 128, 128], P('row', 'col'), may hold values from -6 to 6
- factors: bfloat16 [8, 16, 256, 128, 128], P('row', 'col', 'vc'), may hold values from -0.125 to 0.125
- pno_counts: int32 [32, 32], P('row', 'col'), may hold values from 32 to 128, as said below
- pair_live: int32 [32, 32], P('row', 'col'), may hold values from 0 to 1, as said below
Outputs:
- residual_ladder: float32 [32, 32, 128, 128], P('row', 'col', 'vc')
Inputs may be any that keep to these rules, and one draw needn't show every extreme that they name: pno_counts[i, j] equals pno_counts[j, i]; every diagonal entry is 128. pair_live[i, j] equals pair_live[j, i]; every diagonal entry is 1.
All inputs are finite; a program needn't handle non-finite values.
Results may differ from a plain program's by a relative error of at most 0.0028.
Values sent between devices are 32-bit elements; how exact they have to be, the bound alone decides.
A program may use at most 64 MiB of HBM per device.

v0:
```python
import jax
import jax.numpy as jnp
from jax import lax
from jax.sharding import PartitionSpec as P


def ladder_tile(domain, masked):
    half_tile = jnp.einsum(
        "qac,cd->qad", domain, masked, preferred_element_type=jnp.float32
    ).astype(jnp.bfloat16)
    return jnp.einsum("qad,qbd->ab", half_tile, domain, preferred_element_type=jnp.float32)


def mirrored_pairs(payload):
    row_slots, col_slots, height, breadth = payload.shape
    sectioned = payload.reshape(2, row_slots // 2, col_slots, height, breadth)
    arrived = lax.all_to_all(
        lax.all_to_all(sectioned, "row", split_axis=3, concat_axis=0, tiled=True),
        "col",
        split_axis=0,
        concat_axis=0,
        tiled=True,
    )
    arrived = lax.all_to_all(arrived, "row", split_axis=0, concat_axis=3, tiled=True)
    return jnp.transpose(arrived, (0, 2, 1, 3, 4)).reshape(row_slots, col_slots, height, breadth)


def on_device(amplitudes, factors, pno_counts, pair_live):
    row_slots, col_slots, virtuals = (amplitudes.shape[0], amplitudes.shape[1], amplitudes.shape[2])
    domain = factors[0, 0]
    positions = lax.broadcasted_iota(jnp.int32, (virtuals,), 0)
    pair_tiles = []
    for row_slot in range(row_slots):
        for col_slot in range(col_slots):
            inside = (positions < pno_counts[row_slot, col_slot]).astype(jnp.bfloat16)
            masked = amplitudes[row_slot, col_slot] * inside[:, None] * inside[None, :]
            ladder_term = ladder_tile(domain, masked)
            pair_tiles.append(ladder_term)
    partials = jnp.stack(pair_tiles).reshape(row_slots, col_slots, virtuals, virtuals)
    slab_rows = virtuals // lax.axis_size("vc")
    vc_index = lax.axis_index("vc")
    ladder_sum = lax.psum(partials, "vc")
    own_rows = lax.dynamic_slice_in_dim(ladder_sum, vc_index * slab_rows, slab_rows, 2)
    flipped = jnp.swapaxes(
        lax.dynamic_slice_in_dim(ladder_sum, vc_index * slab_rows, slab_rows, 3), 2, 3
    )
    summed = own_rows + mirrored_pairs(flipped)
    rows_here = vc_index * slab_rows + lax.broadcasted_iota(jnp.int32, (slab_rows,), 0)
    inside_rows = rows_here[None, None, :] < pno_counts[:, :, None]
    inside_cols = positions[None, None, :] < pno_counts[:, :, None]
    kept_cells = (
        inside_rows[:, :, :, None] & inside_cols[:, :, None, :] & (pair_live[:, :, None, None] > 0)
    )
    return jnp.where(kept_cells, summed, jnp.zeros_like(summed))


def solution(mesh):
    in_specs = (
        P("row", "col", None, None),
        P("row", "col", "vc", None, None),
        P("row", "col"),
        P("row", "col"),
    )
    out_specs = P("row", "col", "vc", None)
    return jax.shard_map(
        on_device, mesh=mesh, in_specs=in_specs, out_specs=out_specs, check_vma=False
    )
```

profile of v0, /device:TPU:2, one launch (start us, length us, event | category | flops | bytes accessed | tf_op | source)
XLA Modules:
  0.0 149.3 jit_solution(5824336082564889503)
XLA Ops:
  6.5 1.7 %fusion.289 = (s32[1,1]{0,1:T(1,128)}, s32[1,1]{0,1:T(1,128)}, s32[1,1]{0,1:T(1,128)}, s32[1,1]{0,1:T(1,128)}, s32[1,1]{0,1:T(1,128)}, /*index=5*/s32[1,1]{0,1:T(1,128)}, s32[1,1]{0,1:T(1,128)}, s32[1,1]{0,1:T(1,128)}) fusion(s32[4,2]{0,1:T(2,128)} %param.6), kind=kLoop, calls=%fused_computation.127 | loop fusion | bytes 64 | tf_op jit(solution)/shard_map/slice | solution.py:35
  10.7 0.6 compare_convert_fusion.3
  11.9 0.7 compare_convert_fusion.1
  12.6 0.7 compare_convert_fusion
  13.3 2.6 %fusion.87 = f32[8,128,128]{2,1,0:T(8,128)S(1)} fusion(bf16[1,1,64,128,128]{4,3,2,1,0:T(8,128)(2,1)S(1)} %copy-done, bf16[4,2,128,128]{3,2,1,0:T(8,128)(2,1)} %param.4, bf16[128]{0:T(256)(128)(2,1)S(1)} %compare_convert_fusion.7), kind=kOutput, calls=%fused_computation.49 | convolution fusion | flops 538017792 | bytes 4293632 | tf_op jit(solution)/shard_map/qad,qbd->ab/dot_general | solution.py:11
  15.9 1.8 %fusion.101 = f32[8,128,128]{2,1,0:T(8,128)S(1)} fusion(f32[8,128,128]{2,1,0:T(8,128)S(1)} %fusion.87, bf16[1,1,64,128,128]{4,3,2,1,0:T(8,128)(2,1)S(1)} %copy-done, bf16[4,2,128,128]{3,2,1,0:T(8,128)(2,1)S(1)} %copy-done.2, bf16[128]{0:T(256)(128)(2,1)S(1)} %compare_convert_fusion.6), kind=kOutput, calls=%fused_computation.51 | convolution fusion | flops 538017792 | bytes 4293632 | tf_op jit(solution)/shard_map/qad,qbd->ab/dot_general | solution.py:11
  17.7 1.8 %fusion.115 = f32[8,128,128]{2,1,0:T(8,128)S(1)} fusion(f32[8,128,128]{2,1,0:T(8,128)S(1)} %fusion.101, bf16[1,1,64,128,128]{4,3,2,1,0:T(8,128)(2,1)S(1)} %copy-done, bf16[4,2,128,128]{3,2,1,0:T(8,128)(2,1)S(1)} %copy-done.2, bf16[128]{0:T(256)(128)(2,1)S(1)} %compare_convert_fusion.5), kind=kOutput, calls=%fused_computation.53 | convolution fusion | flops 538017792 | bytes 4293632 | tf_op jit(solution)/shard_map/qad,qbd->ab/dot_general | solution.py:11
  19.5 1.8 %fusion.129 = f32[8,128,128]{2,1,0:T(8,128)S(1)} fusion(f32[8,128,128]{2,1,0:T(8,128)S(1)} %fusion.115, bf16[1,1,64,128,128]{4,3,2,1,0:T(8,128)(2,1)S(1)} %copy-done, bf16[4,2,128,128]{3,2,1,0:T(8,128)(2,1)S(1)} %copy-done.2, bf16[128]{0:T(256)(128)(2,1)S(1)} %compare_convert_fusion.4), kind=kOutput, calls=%fused_computation.55 | convolution fusion | flops 538017792 | bytes 4293632 | tf_op jit(solution)/shard_map/qad,qbd->ab/dot_general | solution.py:11
  21.2 1.8 %fusion.143 = f32[8,128,128]{2,1,0:T(8,128)S(1)} fusion(f32[8,128,128]{2,1,0:T(8,128)S(1)} %fusion.129, bf16[1,1,64,128,128]{4,3,2,1,0:T(8,128)(2,1)S(1)} %copy-done, bf16[4,2,128,128]{3,2,1,0:T(8,128)(2,1)S(1)} %copy-done.2, bf16[128]{0:T(256)(128)(2,1)S(1)} %compare_convert_fusion.3), kind=kOutput, calls=%fused_computation.57 | convolution fusion | flops 538017792 | bytes 4293632 | tf_op jit(solution)/shard_map/qad,qbd->ab/dot_general | solution.py:11
  23.0 1.8 %fusion.157 = f32[8,128,128]{2,1,0:T(8,128)S(1)} fusion(f32[8,128,128]{2,1,0:T(8,128)S(1)} %fusion.143, bf16[1,1,64,128,128]{4,3,2,1,0:T(8,128)(2,1)S(1)} %copy-done, bf16[4,2,128,128]{3,2,1,0:T(8,128)(2,1)S(1)} %copy-done.2, bf16[128]{0:T(256)(128)(2,1)S(1)} %compare_convert_fusion.2), kind=kOutput, calls=%fused_computation.59 | convolution fusion | flops 538017792 | bytes 4293632 | tf_op jit(solution)/shard_map/qad,qbd->ab/dot_general | solution.py:11
  24.8 1.8 %fusion.171 = f32[8,128,128]{2,1,0:T(8,128)S(1)} fusion(f32[8,128,128]{2,1,0:T(8,128)S(1)} %fusion.157, bf16[1,1,64,128,128]{4,3,2,1,0:T(8,128)(2,1)S(1)} %copy-done, bf16[4,2,128,128]{3,2,1,0:T(8,128)(2,1)S(1)} %copy-done.2, bf16[128]{0:T(256)(128)(2,1)S(1)} %compare_convert_fusion.1), kind=kOutput, calls=%fused_computation.61 | convolution fusion | flops 538017792 | bytes 4293632 | tf_op jit(solution)/shard_map/qad,qbd->ab/dot_general | solution.py:11
  26.6 1.8 %fusion.185 = f32[8,128,128]{2,1,0:T(8,128)S(1)} fusion(f32[8,128,128]{2,1,0:T(8,128)S(1)} %fusion.171, bf16[1,1,64,128,128]{4,3,2,1,0:T(8,128)(2,1)S(1)} %copy-done, bf16[4,2,128,128]{3,2,1,0:T(8,128)(2,1)S(1)} %copy-done.2, bf16[128]{0:T(256)(128)(2,1)S(1)} %compare_convert_fusion), kind=kOutput, calls=%fused_computation.63 | convolution fusion | flops 538017792 | bytes 4293632 | tf_op jit(solution)/shard_map/qad,qbd->ab/dot_general | solution.py:11
  28.5 0.8 copy-done.1
  29.3 61.2 %all-reduce.2.cloned.1.call-done = f32[4,2,128,128]{3,2,1,0:T(8,128)} async-done(((f32[4,2,128,128]{3,2,1,0:T(8,128)}), f32[4,2,128,128]{3,2,1,0:T(8,128)}) %all-reduce.2.cloned.1.call-update) | async-done | bytes 524304 | tf_op jit(solution)/shard_map/psum | solution.py:42
  90.5 1.2 constant_dynamic-slice_fusion
  91.7 0.8 copy.77
  92.6 5.7 %all-to-all-start = ((f32[2,2,2,32,128]{4,2,1,0,3:T(2,128)}), f32[2,2,2,32,128]{4,2,1,0,3:T(2,128)S(1)}, u32[]{:S(2)}, u32[]{:S(2)}) async-start(f32[2,2,2,32,128]{4,2,1,0,3:T(2,128)} %copy.77), calls=%async_computation | async-start | bytes 262144 | tf_op jit(solution)/shard_map/all_to_all | solution.py:18
  98.4 5.1 %all-to-all-done = f32[2,2,2,32,128]{4,2,1,0,3:T(2,128)S(1)} async-done(((f32[2,2,2,32,128]{4,2,1,0,3:T(2,128)}), f32[2,2,2,32,128]{4,2,1,0,3:T(2,128)S(1)}, u32[]{:S(2)}, u32[]{:S(2)}) %all-to-all-start) | async-done | bytes 131104 | tf_op jit(solution)/shard_map/all_to_all | solution.py:18
  103.7 0.7 copy.80
  104.4 12.3 %all-to-all-start.1 = ((f32[16,2,2,4,128]{4,3,2,1,0:T(4,128)}), f32[16,2,2,4,128]{4,3,2,1,0:T(4,128)}, u32[]{:S(2)}, u32[]{:S(2)}) async-start(f32[16,2,2,4,128]{4,3,2,1,0:T(4,128)} %copy.80), calls=%async_computation.1 | async-start | bytes 262144 | tf_op jit(solution)/shard_map/all_to_all | solution.py:17
  117.0 13.8 %all-to-all-done.1 = f32[16,2,2,4,128]{4,3,2,1,0:T(4,128)} async-done(((f32[16,2,2,4,128]{4,3,2,1,0:T(4,128)}), f32[16,2,2,4,128]{4,3,2,1,0:T(4,128)}, u32[]{:S(2)}, u32[]{:S(2)}) %all-to-all-start.1) | async-done | bytes 131104 | tf_op jit(solution)/shard_map/all_to_all | solution.py:17
  130.8 4.6 %all-to-all-start.2 = ((f32[16,2,2,4,128]{4,3,2,1,0:T(4,128)}), f32[16,2,2,4,128]{4,3,2,1,0:T(4,128)S(1)}, u32[]{:S(2)}, u32[]{:S(2)}) async-start(f32[16,2,2,4,128]{4,3,2,1,0:T(4,128)} %all-to-all-done.1), calls=%async_computation.2 | async-start | bytes 262144 | tf_op jit(solution)/shard_map/all_to_all | solution.py:24
  135.4 5.2 %all-to-all-done.2 = f32[16,2,2,4,128]{4,3,2,1,0:T(4,128)S(1)} async-done(((f32[16,2,2,4,128]{4,3,2,1,0:T(4,128)}), f32[16,2,2,4,128]{4,3,2,1,0:T(4,128)S(1)}, u32[]{:S(2)}, u32[]{:S(2)}) %all-to-all-start.2) | async-done | bytes 131104 | tf_op jit(solution)/shard_map/all_to_all | solution.py:24
  140.7 1.7 %fusion.192 = f32[4,2,32,128]{3,2,1,0:T(8,128)} fusion(f32[2,2,2,32,128]{4,3,2,1,0:T(8,128)S(1)} %copy.83, f32[4,2,128,128]{3,2,1,0:T(8,128)} %all-reduce.2.cloned.1.call-done, s32[]{:T(128)S(6)} %select_n.8, pred[4,2]{1,0:T(4,128)(4,1)S(1)} %copy.60, pred[4,2,128]{2,1,0:T(4,128)(4,1)S(1)} %iota_compare_fusion, pred[4,2,32]{2,1,0:T(4,128)(4,1)S(1)} %broadcast_compare_fusion), kind=kLoop, calls=%fused_computation.65 | loop fusion | flops 131072 | bytes 394508 | tf_op jit(solution)/shard_map/jit(_where)/select_n | solution.py:54
  (27 shorter events, 3.6 us)
Async XLA Ops:
  6.5 6.7 %copy-start = (bf16[1,1,64,128,128]{4,3,2,1,0:T(8,128)(2,1)S(1)}, bf16[1,1,64,128,128]{4,3,2,1,0:T(8,128)(2,1)}, u32[]{:S(2)}) copy-start(bf16[1,1,64,128,128]{4,3,2,1,0:T(8,128)(2,1)} %param.5) | copy-start | bytes 6291460
  6.5 83.9 %all-reduce.2.cloned.1.call-start = ((), (), s32[]{:S(2)}) async-start(), calls=%async_computation.3 | async-start | bytes 1048576 | tf_op jit(solution)/shard_map/psum | solution.py:42
  13.2 2.6 %copy-start.2 = (bf16[4,2,128,128]{3,2,1,0:T(8,128)(2,1)S(1)}, bf16[4,2,128,128]{3,2,1,0:T(8,128)(2,1)}, u32[]{:S(2)}) copy-start(bf16[4,2,128,128]{3,2,1,0:T(8,128)(2,1)} %param.4) | copy-start | bytes 786436
  28.4 0.8 copy-start.1
  28.5 69.9 %copy-start.3 = (s32[4,2]{0,1:T(2,128)S(1)}, s32[4,2]{0,1:T(2,128)}, u32[]{:S(2)}) copy-start(s32[4,2]{0,1:T(2,128)} %param.6) | copy-start | bytes 100
  28.5 88.3 %copy-start.4 = (s32[4,2]{0,1:T(2,128)S(1)}, s32[4,2]{0,1:T(2,128)}, u32[]{:S(2)}) copy-start(s32[4,2]{0,1:T(2,128)} %param.7) | copy-start | bytes 100
  92.6 11.0 %all-to-all-start = ((f32[2,2,2,32,128]{4,2,1,0,3:T(2,128)}), f32[2,2,2,32,128]{4,2,1,0,3:T(2,128)S(1)}, u32[]{:S(2)}, u32[]{:S(2)}) async-start(f32[2,2,2,32,128]{4,2,1,0,3:T(2,128)} %copy.77), calls=%async_computation | async-start | bytes 262144 | tf_op jit(solution)/shard_map/all_to_all | solution.py:18
  104.4 26.4 %all-to-all-start.1 = ((f32[16,2,2,4,128]{4,3,2,1,0:T(4,128)}), f32[16,2,2,4,128]{4,3,2,1,0:T(4,128)}, u32[]{:S(2)}, u32[]{:S(2)}) async-start(f32[16,2,2,4,128]{4,3,2,1,0:T(4,128)} %copy.80), calls=%async_computation.1 | async-start | bytes 262144 | tf_op jit(solution)/shard_map/all_to_all | solution.py:17
  130.8 9.8 %all-to-all-start.2 = ((f32[16,2,2,4,128]{4,3,2,1,0:T(4,128)}), f32[16,2,2,4,128]{4,3,2,1,0:T(4,128)S(1)}, u32[]{:S(2)}, u32[]{:S(2)}) async-start(f32[16,2,2,4,128]{4,3,2,1,0:T(4,128)} %all-to-all-done.1), calls=%async_computation.2 | async-start | bytes 262144 | tf_op jit(solution)/shard_map/all_to_all | solution.py:24
Sparse Core Ops, SparseCore 0:
  29.4 61.0 all-reduce.1
where the time goes:
time: 150 us; the launch traced here: 149 us
  waiting for transfers between devices  85.4 us (57%)
  starting transfers between devices  22.6 us (15%)
  matrix products  15.1 us (10%)
  between operations  13.6 us (9%)
  other arithmetic  6.83 us (5%)
  local copies, waits for them, and re-layouts  5.67 us (4%)
    psum x1, waiting for transfers between devices, on_device(): ladder_sum = lax.psum(partials, 'vc')  61.2 us
    dot_general x8, matrix products, ladder_tile(): jnp.einsum('qad,qbd->ab', half_tile, domain, preferred_element_type=jnp.f...  15.1 us
    all_to_all x1, waiting for transfers between devices, mirrored_pairs(): lax.all_to_all(lax.all_to_all(sectioned, 'row', split_axis=3, concat_axis...  13.8 us
    all_to_all x1, starting transfers between devices, mirrored_pairs(): lax.all_to_all(lax.all_to_all(sectioned, 'row', split_axis=3, concat_axis...  12.3 us
    all_to_all x1, starting transfers between devices, mirrored_pairs(): lax.all_to_all(sectioned, 'row', split_axis=3, concat_axis=0, tiled=True)  5.75 us
    all_to_all x1, waiting for transfers between devices, mirrored_pairs(): lax.all_to_all(arrived, 'row', split_axis=0, concat_axis=3, tiled=True)  5.18 us
    all_to_all x1, waiting for transfers between devices, mirrored_pairs(): lax.all_to_all(sectioned, 'row', split_axis=3, concat_axis=0, tiled=True)  5.14 us
    convert_element_type x8, other arithmetic, on_device(): inside = (positions < pno_counts[row_slot, col_slot]).astype(jnp.bfloat16)  4.98 us
  transfers between devices with their start and end apart: 4, of which 4 were waited for; matrix products, arithmetic and copies ran while one was open for 0% of the time, Pallas kernels for 0%

commit v1 on v0

v1 whole, which is shorter than its diff:
```python
import jax
import jax.numpy as jnp
from jax import lax
from jax.experimental import pallas as pl
from jax.experimental.pallas import tpu as pltpu
from jax.sharding import PartitionSpec as P

MESH = pl.DeviceIdType.MESH
VIRT = 128
AUX = 64
SLAB = 32
QC = 32
LOADS = 4


def shift(row, bx, dy):
    return ((row // 4 + bx) % 2) * 4 + (row % 4 + dy) % 4


ROUTES = [(h, vd, vd % 2, 2 * (vd // 2) + h) for h in range(2) for vd in range(4)]


def kernel(
    amps,
    factors,
    counts,
    live,
    out,
    raw,
    fac,
    masked,
    acc,
    part,
    part_in,
    own,
    turned,
    relay,
    mirror,
    amp_sem,
    fac_sem,
    part_send,
    part_recv,
    relay_send,
    relay_recv,
    mirror_send,
    mirror_recv,
):
    R = lax.axis_index("row")
    z = lax.axis_index("col")
    v = lax.axis_index("vc")
    k = z % 2
    x_hi, core = v // 2, v % 2
    peers = {1: v + 1 - 2 * core, 2: (v + 2) % 4, 3: 3 - v}

    amp_copy = pltpu.make_async_copy(amps, raw, amp_sem)
    amp_copy.start()
    step_q = AUX // LOADS
    fac_copies = [
        pltpu.make_async_copy(
            factors.at[0, 0, pl.ds(n * step_q, step_q)],
            fac.at[pl.ds(n * step_q, step_q)],
            fac_sem.at[n],
        )
        for n in range(LOADS)
    ]
    for copy in fac_copies:
        copy.start()

    barrier = pltpu.get_barrier_semaphore()
    waits = 0
    for d in (1, 2, 3):
        pl.semaphore_signal(barrier, inc=1, device_id=(R, z, peers[d]), device_id_type=MESH)
        waits += 1
    for _, _, bx, dy in ROUTES:
        if bx or dy:
            pl.semaphore_signal(
                barrier, inc=1, device_id=(shift(R, bx, 4 - dy), z, v), device_id_type=MESH
            )
            waits += 1
    bx_in, dy_in = v % 2, 2 * (v // 2) + k
    row_in = shift(z // 2, bx_in, dy_in)
    for vs in range(4):
        for ks in range(2):
            not_here = jnp.logical_not((row_in == R) & (2 * R + ks == z) & (v == vs))

            @pl.when(not_here)
            def _():
                pl.semaphore_signal(
                    barrier, inc=1, device_id=(row_in, 2 * R + ks, vs), device_id_type=MESH
                )

            waits = waits + not_here.astype(jnp.int32)

    amp_copy.wait()
    rows = lax.broadcasted_iota(jnp.int32, (VIRT, VIRT), 0)
    cols = lax.broadcasted_iota(jnp.int32, (VIRT, VIRT), 1)
    reach = jnp.maximum(rows, cols)
    for s in range(4):
        for t in range(2):
            g, p = s // 2, (s % 2) * 2 + t
            tile = jnp.where(reach < counts[s, t], raw[s, t].astype(jnp.float32), 0.0)
            masked[g, :, p * VIRT : (p + 1) * VIRT] = tile.astype(jnp.bfloat16)
    for copy in fac_copies:
        copy.wait()

    def part_copy(g, d):
        src = part.at[g, 1, 1 - core] if d == 1 else part.at[g, 0, core if d == 2 else 1 - core]
        return pltpu.make_async_remote_copy(
            src_ref=src,
            dst_ref=part_in.at[g, d - 1],
            send_sem=part_send.at[g, d - 1],
            recv_sem=part_recv.at[g, d - 1],
            device_id=(R, z, peers[d]),
            device_id_type=MESH,
        )

    def relay_copy(h, vd, bx, dy):
        i = h * 4 + vd
        return pltpu.make_async_remote_copy(
            src_ref=turned.at[i],
            dst_ref=relay.at[i],
            send_sem=relay_send.at[i],
            recv_sem=relay_recv.at[i],
            device_id=(shift(R, bx, dy), z, v),
            device_id_type=MESH,
        )

    def last_leg(h, vd, bx, dy):
        i = h * 4 + vd
        row_from = shift(R, bx, 4 - dy)
        here = (z // 2 == R) & (2 * row_from + h == z) & (v == vd)
        src = relay if bx or dy else turned

        def remote():
            return pltpu.make_async_remote_copy(
                src_ref=src.at[i],
                dst_ref=mirror.at[v, k],
                send_sem=mirror_send.at[i],
                recv_sem=mirror_recv.at[v, k],
                device_id=(z // 2, 2 * row_from + h, vd),
                device_id_type=MESH,
            )

        def local():
            return pltpu.make_async_copy(src.at[i], mirror.at[v, k], mirror_recv.at[v, k])

        return here, remote, local

    def reduce_and_turn(g):
        for d in (1, 2, 3):
            part_copy(g, d).wait_recv()
        total = part[g, 1, core] + part_in[g, 0] + part_in[g, 1] + part_in[g, 2]
        own[g] = total
        flat = jnp.transpose(total)
        for vd in range(4):
            turned[g * 4 + vd] = flat[vd * SLAB : (vd + 1) * SLAB]
        for h, vd, bx, dy in ROUTES:
            if h == g and (bx or dy):
                relay_copy(h, vd, bx, dy).start()
        for h, vd, bx, dy in ROUTES:
            if h == g and not (bx or dy):
                start_last_leg(h, vd, bx, dy)

    def start_last_leg(h, vd, bx, dy):
        here, remote, local = last_leg(h, vd, bx, dy)

        @pl.when(here)
        def _():
            local().start()

        @pl.when(jnp.logical_not(here))
        def _():
            remote().start()

    def forward(g):
        for h, vd, bx, dy in ROUTES:
            if h == g and (bx or dy):
                relay_copy(h, vd, bx, dy).wait_recv()
                start_last_leg(h, vd, bx, dy)

    def body(j, carry):
        step, q0 = j // 2, (j % 2) * QC
        g, near = step // 2, step % 2
        half = x_hi * near + (1 - x_hi) * (1 - near)
        first_row = pl.multiple_of(half * 2 * SLAB, 2 * SLAB)
        domain = fac[pl.ds(q0, QC)]
        lhs = fac[pl.ds(q0, QC), pl.ds(first_row, 2 * SLAB), :].reshape(QC * 2 * SLAB, VIRT)
        mid = jnp.dot(lhs, masked[g], preferred_element_type=jnp.float32).astype(jnp.bfloat16)
        height = 2 * SLAB
        wide = jnp.concatenate(
            [
                jnp.concatenate(
                    [
                        mid[q * height : (q + 1) * height, p * VIRT : (p + 1) * VIRT]
                        for q in range(QC)
                    ],
                    axis=1,
                )
                for p in range(4)
            ],
            axis=0,
        )
        flat = jnp.concatenate([domain[q] for q in range(QC)], axis=1)
        term = lax.dot_general(
            wide, flat, (((1,), (1,)), ((), ())), preferred_element_type=jnp.float32
        )

        @pl.when(j % 2 == 0)
        def _():
            acc[...] = term

        @pl.when(j % 2 == 1)
        def _():
            total = acc[...] + term
            for c in range(2):
                for p in range(4):
                    at = p * height + c * SLAB
                    part[g, near, c, p * SLAB : (p + 1) * SLAB, :] = total[at : at + SLAB]

        return carry

    def with_sends(j, carry):
        body(j, carry)

        @pl.when(j == 5)
        def _():
            part_copy(1, 2).start()
            part_copy(1, 3).start()

        for gg in range(2):

            @pl.when(j == 4 * gg + 3)
            def _():
                part_copy(gg, 1).start()

        @pl.when(j == 4)
        def _():
            reduce_and_turn(0)

        @pl.when(j == 6)
        def _():
            forward(0)

        return carry

    lax.fori_loop(0, 2, body, 0)
    pl.semaphore_wait(barrier, waits)
    part_copy(0, 2).start()
    part_copy(0, 3).start()
    lax.fori_loop(2, 8, with_sends, 0)
    reduce_and_turn(1)
    forward(1)

    row_ids = v * SLAB + lax.broadcasted_iota(jnp.int32, (SLAB, VIRT), 0)
    col_ids = lax.broadcasted_iota(jnp.int32, (SLAB, VIRT), 1)
    reach_out = jnp.maximum(row_ids, col_ids)
    for ks in range(2):
        for vs in range(4):
            pltpu.make_async_copy(
                mirror.at[vs, ks], mirror.at[vs, ks], mirror_recv.at[vs, ks]
            ).wait()
        pieces = [mirror[vs, ks] for vs in range(4)]
        for sl in range(2):
            for t in range(2):
                p_own, p_in = sl * 2 + t, t * 2 + sl
                flipped = jnp.zeros((SLAB, VIRT), jnp.float32)
                for vs in range(4):
                    turn = ((vs - p_in) % 4) * SLAB
                    moved = pltpu.roll(pieces[vs], turn, 1) if turn else pieces[vs]
                    flipped = jnp.where(col_ids // SLAB == vs, moved, flipped)
                s = 2 * ks + sl
                summed = own[ks, p_own * SLAB : (p_own + 1) * SLAB, :] + flipped
                limit = jnp.where(live[s, t] > 0, counts[s, t], 0)
                out[s, t] = jnp.where(reach_out < limit, summed, 0.0)

    for g in range(2):
        for d in (1, 2, 3):
            part_copy(g, d).wait_send()
    for h, vd, bx, dy in ROUTES:
        if bx or dy:
            relay_copy(h, vd, bx, dy).wait_send()
        here, remote, _ = last_leg(h, vd, bx, dy)

        @pl.when(jnp.logical_not(here))
        def _():
            remote().wait_send()


def on_device(amplitudes, factors, pno_counts, pair_live):
    dma = pltpu.SemaphoreType.DMA
    tile = (4 * SLAB, VIRT)
    return pl.pallas_call(
        kernel,
        out_shape=jax.ShapeDtypeStruct((4, 2, SLAB, VIRT), jnp.float32),
        in_specs=[
            pl.BlockSpec(memory_space=pl.ANY),
            pl.BlockSpec(memory_space=pl.ANY),
            pl.BlockSpec(memory_space=pltpu.SMEM),
            pl.BlockSpec(memory_space=pltpu.SMEM),
        ],
        out_specs=pl.BlockSpec(memory_space=pltpu.VMEM),
        scratch_shapes=[
            pltpu.VMEM((4, 2, VIRT, VIRT), jnp.bfloat16),
            pltpu.VMEM((AUX, VIRT, VIRT), jnp.bfloat16),
            pltpu.VMEM((2, VIRT, 4 * VIRT), jnp.bfloat16),
            pltpu.VMEM((8 * SLAB, VIRT), jnp.float32),
            pltpu.VMEM((2, 2, 2) + tile, jnp.float32),
            pltpu.VMEM((2, 3) + tile, jnp.float32),
            pltpu.VMEM((2,) + tile, jnp.float32),
            pltpu.VMEM((8, SLAB, VIRT), jnp.float32),
            pltpu.VMEM((8, SLAB, VIRT), jnp.float32),
            pltpu.VMEM((4, 2, SLAB, VIRT), jnp.float32),
            dma,
            dma((LOADS,)),
            dma((2, 3)),
            dma((2, 3)),
            dma((8,)),
            dma((8,)),
            dma((8,)),
            dma((4, 2)),
        ],
        compiler_params=pltpu.CompilerParams(
            collective_id=0, has_side_effects=True, vmem_limit_bytes=48 << 20
        ),
        name="ladder",
    )(amplitudes, factors, pno_counts, pair_live)


def solution(mesh):
    in_specs = (
        P("row", "col", None, None),
        P("row", "col", "vc", None, None),
        P("row", "col"),
        P("row", "col"),
    )
    out_specs = P("row", "col", "vc", None)
    return jax.shard_map(
        on_device, mesh=mesh, in_specs=in_specs, out_specs=out_specs, check_vma=False
    )
```

time: 150 us -> 50 us (0.33)
  the two profiles are of different devices: /device:TPU:2 before, /device:TPU:49 now
where the time goes in v1:
time: 50 us; the launch traced here: 49.8 us
  Pallas kernels  45 us (90%)
  local copies, waits for them, and re-layouts  4.73 us (9%)
    pallas_call x1, Pallas kernels, on_device(): pl.pallas_call(kernel, out_shape=jax.ShapeDtypeStruct((4, 2, SLAB, VIRT),...  45 us
    unnamed x7, local copies, waits for them, and re-layouts  4.73 us

profile of v1, /device:TPU:49, one launch (start us, length us, event | category | flops | bytes accessed | tf_op | source)
XLA Modules:
  0.0 49.8 jit_solution(13213024118361566494)
XLA Ops:
  0.0 0.8 %copy.5.counts = s32[4,2]{1,0:T(4,128)S(1)} copy(s32[4,2]{0,1:T(2,128)} %param.6) | data formatting | bytes 64 | tf_op args[2]
  0.8 0.8 %copy.6.live = s32[4,2]{1,0:T(4,128)S(1)} copy(s32[4,2]{0,1:T(2,128)} %param.7) | data formatting | bytes 64 | tf_op args[3]
  1.5 0.0 copy-start
  1.5 1.6 %copy-done = bf16[1,1,64,128,128]{4,3,2,1,0:T(8,128)(2,1)S(1)} copy-done((bf16[1,1,64,128,128]{4,3,2,1,0:T(8,128)(2,1)S(1)}, bf16[1,1,64,128,128]{4,3,2,1,0:T(8,128)(2,1)}, u32[]{:S(2)}) %copy-start) | copy-done | bytes 2097176
  3.1 0.0 copy-start.1
  3.1 0.9 %copy-done.1 = bf16[4,2,128,128]{3,2,1,0:T(8,128)(2,1)S(1)} copy-done((bf16[4,2,128,128]{3,2,1,0:T(8,128)(2,1)S(1)}, bf16[4,2,128,128]{3,2,1,0:T(8,128)(2,1)}, u32[]{:S(2)}) %copy-start.1) | copy-done | bytes 262168
  4.1 45.0 %ladder.1 = f32[4,2,32,128]{3,2,1,0:T(8,128)S(1)} custom-call(bf16[4,2,128,128]{3,2,1,0:T(8,128)(2,1)S(1)} %copy-done.1, bf16[1,1,64,128,128]{4,3,2,1,0:T(8,128)(2,1)S(1)} %copy-done, s32[4,2]{1,0:T(4,128)S(1)} %copy.5.counts, s32[4,2]{1,0:T(4,128)S(1)} %copy.6.live), custom_call_target="tpu_custom_call" | custom-call | tf_op jit(solution)/shard_map/ladder/pallas_call | solution.py:292
  49.1 0.7 %copy.8 = f32[4,2,32,128]{3,2,1,0:T(8,128)} copy(f32[4,2,32,128]{3,2,1,0:T(8,128)S(1)} %ladder.1) | data formatting | bytes 262144
Async XLA Ops:
  1.5 1.6 %copy-start = (bf16[1,1,64,128,128]{4,3,2,1,0:T(8,128)(2,1)S(1)}, bf16[1,1,64,128,128]{4,3,2,1,0:T(8,128)(2,1)}, u32[]{:S(2)}) copy-start(bf16[1,1,64,128,128]{4,3,2,1,0:T(8,128)(2,1)} %factors.1) | copy-start | bytes 6291460
  3.1 0.9 %copy-start.1 = (bf16[4,2,128,128]{3,2,1,0:T(8,128)(2,1)S(1)}, bf16[4,2,128,128]{3,2,1,0:T(8,128)(2,1)}, u32[]{:S(2)}) copy-start(bf16[4,2,128,128]{3,2,1,0:T(8,128)(2,1)} %amps.1) | copy-start | bytes 786436

commit v2 on v1

--- a/solution.py
+++ b/solution.py
@@ -17,15 +17,21 @@
     return ((row // 4 + bx) % 2) * 4 + (row % 4 + dy) % 4
 
 
-ROUTES = [(h, vd, vd % 2, 2 * (vd // 2) + h) for h in range(2) for vd in range(4)]
+def route(h, vd):
+    return vd % 2, vd // 2
+
+
+ROUTES = [(h, vd) + route(h, vd) for h in range(2) for vd in range(4)]
 
 
 def kernel(
     amps,
     factors,
+    counts_in,
+    live_in,
+    out,
     counts,
     live,
-    out,
     raw,
     fac,
     masked,
@@ -36,6 +42,7 @@
     turned,
     relay,
     mirror,
+    small_sem,
     amp_sem,
     fac_sem,
     part_send,
@@ -54,6 +61,12 @@
 
     amp_copy = pltpu.make_async_copy(amps, raw, amp_sem)
     amp_copy.start()
+    small_copies = [
+        pltpu.make_async_copy(counts_in, counts, small_sem.at[0]),
+        pltpu.make_async_copy(live_in, live, small_sem.at[1]),
+    ]
+    for copy in small_copies:
+        copy.start()
     step_q = AUX // LOADS
     fac_copies = [
         pltpu.make_async_copy(
@@ -77,7 +90,7 @@
                 barrier, inc=1, device_id=(shift(R, bx, 4 - dy), z, v), device_id_type=MESH
             )
             waits += 1
-    bx_in, dy_in = v % 2, 2 * (v // 2) + k
+    bx_in, dy_in = route(k, v)
     row_in = shift(z // 2, bx_in, dy_in)
     for vs in range(4):
         for ks in range(2):
@@ -91,6 +104,8 @@
 
             waits = waits + not_here.astype(jnp.int32)
 
+    for copy in small_copies:
+        copy.wait()
     amp_copy.wait()
     rows = lax.broadcasted_iota(jnp.int32, (VIRT, VIRT), 0)
     cols = lax.broadcasted_iota(jnp.int32, (VIRT, VIRT), 1)
@@ -98,10 +113,8 @@
     for s in range(4):
         for t in range(2):
             g, p = s // 2, (s % 2) * 2 + t
-            tile = jnp.where(reach < counts[s, t], raw[s, t].astype(jnp.float32), 0.0)
+            tile = jnp.where(reach < counts[t, s], raw[s, t].astype(jnp.float32), 0.0)
             masked[g, :, p * VIRT : (p + 1) * VIRT] = tile.astype(jnp.bfloat16)
-    for copy in fac_copies:
-        copy.wait()
 
     def part_copy(g, d):
         src = part.at[g, 1, 1 - core] if d == 1 else part.at[g, 0, core if d == 2 else 1 - core]
@@ -178,15 +191,10 @@
                 relay_copy(h, vd, bx, dy).wait_recv()
                 start_last_leg(h, vd, bx, dy)
 
-    def body(j, carry):
-        step, q0 = j // 2, (j % 2) * QC
-        g, near = step // 2, step % 2
-        half = x_hi * near + (1 - x_hi) * (1 - near)
-        first_row = pl.multiple_of(half * 2 * SLAB, 2 * SLAB)
+    def products(g, first_row, height, q0):
         domain = fac[pl.ds(q0, QC)]
-        lhs = fac[pl.ds(q0, QC), pl.ds(first_row, 2 * SLAB), :].reshape(QC * 2 * SLAB, VIRT)
+        lhs = fac[pl.ds(q0, QC), pl.ds(first_row, height), :].reshape(QC * height, VIRT)
         mid = jnp.dot(lhs, masked[g], preferred_element_type=jnp.float32).astype(jnp.bfloat16)
-        height = 2 * SLAB
         wide = jnp.concatenate(
             [
                 jnp.concatenate(
@@ -201,54 +209,49 @@
             axis=0,
         )
         flat = jnp.concatenate([domain[q] for q in range(QC)], axis=1)
-        term = lax.dot_general(
+        return lax.dot_general(
             wide, flat, (((1,), (1,)), ((), ())), preferred_element_type=jnp.float32
         )
 
-        @pl.when(j % 2 == 0)
-        def _():
-            acc[...] = term
-
-        @pl.when(j % 2 == 1)
-        def _():
-            total = acc[...] + term
-            for c in range(2):
-                for p in range(4):
-                    at = p * height + c * SLAB
-                    part[g, near, c, p * SLAB : (p + 1) * SLAB, :] = total[at : at + SLAB]
-
-        return carry
-
-    def with_sends(j, carry):
-        body(j, carry)
-
-        @pl.when(j == 5)
-        def _():
-            part_copy(1, 2).start()
-            part_copy(1, 3).start()
-
-        for gg in range(2):
-
-            @pl.when(j == 4 * gg + 3)
-            def _():
-                part_copy(gg, 1).start()
-
-        @pl.when(j == 4)
-        def _():
-            reduce_and_turn(0)
-
-        @pl.when(j == 6)
-        def _():
-            forward(0)
-
-        return carry
-
-    lax.fori_loop(0, 2, body, 0)
+    far_row = pl.multiple_of((1 - x_hi) * 2 * SLAB, 2 * SLAB)
+    near_row = pl.multiple_of(x_hi * 2 * SLAB, 2 * SLAB)
+
+    def store_parts(g, near, total):
+        for c in range(2):
+            for p in range(4):
+                at = (2 * p + c) * SLAB
+                part[g, near, c, p * SLAB : (p + 1) * SLAB, :] = total[at : at + SLAB]
+
+    def all_products(g, first_row, height):
+        return lax.fori_loop(
+            0,
+            AUX // QC,
+            lambda n, total: total + products(g, first_row, height, n * QC),
+            jnp.zeros((4 * height, VIRT), jnp.float32),
+        )
+
+    for copy in fac_copies[: LOADS // 2]:
+        copy.wait()
+    acc[...] = products(0, far_row, 2 * SLAB, 0)
+    for copy in fac_copies[LOADS // 2 :]:
+        copy.wait()
+    store_parts(0, 0, acc[...] + products(0, far_row, 2 * SLAB, QC))
     pl.semaphore_wait(barrier, waits)
     part_copy(0, 2).start()
     part_copy(0, 3).start()
-    lax.fori_loop(2, 8, with_sends, 0)
+    store_parts(1, 0, all_products(1, far_row, 2 * SLAB))
+    part_copy(1, 2).start()
+    part_copy(1, 3).start()
+    store_parts(0, 1, all_products(0, near_row, 2 * SLAB))
+    part_copy(0, 1).start()
+    peer_row = pl.multiple_of(near_row + (1 - core) * SLAB, SLAB)
+    part[1, 1, 1 - core] = all_products(1, peer_row, SLAB)
+    part_copy(1, 1).start()
+    reduce_and_turn(0)
+    own_row = pl.multiple_of(near_row + core * SLAB, SLAB)
+    part[1, 1, core] = all_products(1, own_row, SLAB)
     reduce_and_turn(1)
+    forward(0)
     forward(1)
 
     row_ids = v * SLAB + lax.broadcasted_iota(jnp.int32, (SLAB, VIRT), 0)
@@ -270,7 +273,7 @@
                     flipped = jnp.where(col_ids // SLAB == vs, moved, flipped)
                 s = 2 * ks + sl
                 summed = own[ks, p_own * SLAB : (p_own + 1) * SLAB, :] + flipped
-                limit = jnp.where(live[s, t] > 0, counts[s, t], 0)
+                limit = jnp.where(live[t, s] > 0, counts[t, s], 0)
                 out[s, t] = jnp.where(reach_out < limit, summed, 0.0)
 
     for g in range(2):
@@ -287,19 +290,17 @@
 
 
 def on_device(amplitudes, factors, pno_counts, pair_live):
+    arguments = (amplitudes, factors, pno_counts.T, pair_live.T)
     dma = pltpu.SemaphoreType.DMA
     tile = (4 * SLAB, VIRT)
     return pl.pallas_call(
         kernel,
         out_shape=jax.ShapeDtypeStruct((4, 2, SLAB, VIRT), jnp.float32),
-        in_specs=[
-            pl.BlockSpec(memory_space=pl.ANY),
-            pl.BlockSpec(memory_space=pl.ANY),
-            pl.BlockSpec(memory_space=pltpu.SMEM),
-            pl.BlockSpec(memory_space=pltpu.SMEM),
-        ],
+        in_specs=[pl.BlockSpec(memory_space=pltpu.HBM)] * 4,
         out_specs=pl.BlockSpec(memory_space=pltpu.VMEM),
         scratch_shapes=[
+            pltpu.SMEM((2, 4), jnp.int32),
+            pltpu.SMEM((2, 4), jnp.int32),
             pltpu.VMEM((4, 2, VIRT, VIRT), jnp.bfloat16),
             pltpu.VMEM((AUX, VIRT, VIRT), jnp.bfloat16),
             pltpu.VMEM((2, VIRT, 4 * VIRT), jnp.bfloat16),
@@ -310,6 +311,7 @@
             pltpu.VMEM((8, SLAB, VIRT), jnp.float32),
             pltpu.VMEM((8, SLAB, VIRT), jnp.float32),
             pltpu.VMEM((4, 2, SLAB, VIRT), jnp.float32),
+            dma((2,)),
             dma,
             dma((LOADS,)),
             dma((2, 3)),
@@ -323,7 +325,7 @@
             collective_id=0, has_side_effects=True, vmem_limit_bytes=48 << 20
         ),
         name="ladder",
-    )(amplitudes, factors, pno_counts, pair_live)
+    )(*(pltpu.with_memory_space_constraint(a, pltpu.HBM) for a in arguments))
 
 
 def solution(mesh):

time: 50 us -> 38.2 us (0.76)
  the two profiles are of different devices: /device:TPU:49 before, /device:TPU:63 now
where the time goes in v2:
time: 38.2 us; the launch traced here: 38 us
  Pallas kernels  37.4 us (98%)
  local copies, waits for them, and re-layouts  0.66 us (2%)
    pallas_call x1, Pallas kernels, on_device(): pl.pallas_call(kernel, out_shape=jax.ShapeDtypeStruct((4, 2, SLAB, VIRT),...  37.4 us

profile of v2, /device:TPU:63, one launch (start us, length us, event | category | flops | bytes accessed | tf_op | source)
XLA Modules:
  0.0 38.0 jit_solution(963575814623822928)
XLA Ops:
  0.0 37.4 %ladder.1 = f32[4,2,32,128]{3,2,1,0:T(8,128)S(1)} custom-call(bf16[4,2,128,128]{3,2,1,0:T(8,128)(2,1)} %amps.1, bf16[1,1,64,128,128]{4,3,2,1,0:T(8,128)(2,1)} %factors.1, s32[2,4]{1,0:T(2,128)} %bitcast.2, s32[2,4]{1,0:T(2,128)} %bitcast.3), custom_call_target="tpu_custom_call" | custom-call | tf_op jit(solution)/shard_map/ladder/pallas_call | solution.py:296
  37.4 0.7 %copy.6 = f32[4,2,32,128]{3,2,1,0:T(8,128)} copy(f32[4,2,32,128]{3,2,1,0:T(8,128)S(1)} %ladder.1) | data formatting | bytes 262144

commit v3 on v2

--- a/solution.py
+++ b/solution.py
@@ -9,7 +9,8 @@
 VIRT = 128
 AUX = 64
 SLAB = 32
-QC = 32
+QC = 4
+MEETS = (2, 3, 1, 0)
 LOADS = 4
 
 
@@ -35,7 +36,6 @@
     raw,
     fac,
     masked,
-    acc,
     part,
     part_in,
     own,
@@ -222,34 +222,53 @@
                 at = (2 * p + c) * SLAB
                 part[g, near, c, p * SLAB : (p + 1) * SLAB, :] = total[at : at + SLAB]
 
-    def all_products(g, first_row, height):
-        return lax.fori_loop(
-            0,
-            AUX // QC,
-            lambda n, total: total + products(g, first_row, height, n * QC),
-            jnp.zeros((4 * height, VIRT), jnp.float32),
-        )
-
-    for copy in fac_copies[: LOADS // 2]:
+    def sum_products(g, first_row, height, start, stop):
+        total = products(g, first_row, height, start)
+        for q0 in range(start + QC, stop, QC):
+            total = total + products(g, first_row, height, q0)
+        return total
+
+    fresh = (((0, 2), (0, 3)), ((1, 2), (1, 3)), ((0, 1),), ((1, 1),))
+
+    def send_parts(step):
+        @pl.when(z // 4 == MEETS[step])
+        def _():
+            pl.semaphore_wait(barrier, waits)
+            for group in fresh[: step + 1]:
+                for g, d in group:
+                    part_copy(g, d).start()
+
+        for quarter in MEETS[:step]:
+
+            @pl.when(z // 4 == quarter)
+            def _():
+                for g, d in fresh[step]:
+                    part_copy(g, d).start()
+
+    for copy in fac_copies:
         copy.wait()
-    acc[...] = products(0, far_row, 2 * SLAB, 0)
-    for copy in fac_copies[LOADS // 2 :]:
-        copy.wait()
-    store_parts(0, 0, acc[...] + products(0, far_row, 2 * SLAB, QC))
-    pl.semaphore_wait(barrier, waits)
-    part_copy(0, 2).start()
-    part_copy(0, 3).start()
-    store_parts(1, 0, all_products(1, far_row, 2 * SLAB))
-    part_copy(1, 2).start()
-    part_copy(1, 3).start()
-    store_parts(0, 1, all_products(0, near_row, 2 * SLAB))
-    part_copy(0, 1).start()
+    store_parts(0, 0, sum_products(0, far_row, 2 * SLAB, 0, AUX))
+    send_parts(0)
+    store_parts(1, 0, sum_products(1, far_row, 2 * SLAB, 0, AUX))
+    send_parts(1)
     peer_row = pl.multiple_of(near_row + (1 - core) * SLAB, SLAB)
-    part[1, 1, 1 - core] = all_products(1, peer_row, SLAB)
-    part_copy(1, 1).start()
-    reduce_and_turn(0)
     own_row = pl.multiple_of(near_row + core * SLAB, SLAB)
-    part[1, 1, core] = all_products(1, own_row, SLAB)
+    part[0, 1, 1 - core] = sum_products(0, peer_row, SLAB, 0, AUX)
+    send_parts(2)
+    part[0, 1, core] = sum_products(0, own_row, SLAB, 0, AUX)
+
+    @pl.when(z // 4 == MEETS[0])
+    def _():
+        reduce_and_turn(0)
+
+    part[1, 1, 1 - core] = sum_products(1, peer_row, SLAB, 0, AUX)
+    send_parts(3)
+    part[1, 1, core] = sum_products(1, own_row, SLAB, 0, AUX)
+
+    @pl.when(z // 4 != MEETS[0])
+    def _():
+        reduce_and_turn(0)
+
     reduce_and_turn(1)
     forward(0)
     forward(1)
@@ -304,7 +323,6 @@
             pltpu.VMEM((4, 2, VIRT, VIRT), jnp.bfloat16),
             pltpu.VMEM((AUX, VIRT, VIRT), jnp.bfloat16),
             pltpu.VMEM((2, VIRT, 4 * VIRT), jnp.bfloat16),
-            pltpu.VMEM((8 * SLAB, VIRT), jnp.float32),
             pltpu.VMEM((2, 2, 2) + tile, jnp.float32),
             pltpu.VMEM((2, 3) + tile, jnp.float32),
             pltpu.VMEM((2,) + tile, jnp.float32),

time: 38.2 us -> 37.9 us (level)
  Pallas kernels: 37.4 us -> 37 us
where the time goes in v3:
time: 37.9 us; the launch traced here: 37.7 us
  Pallas kernels  37 us (98%)
  local copies, waits for them, and re-layouts  0.66 us (2%)
    pallas_call x1, Pallas kernels, on_device(): pl.pallas_call(kernel, out_shape=jax.ShapeDtypeStruct((4, 2, SLAB, VIRT),...  37 us

profile of v3, /device:TPU:63, one launch (start us, length us, event | category | flops | bytes accessed | tf_op | source)
XLA Modules:
  0.0 37.7 jit_solution(15453284282587714954)
XLA Ops:
  0.0 37.0 %ladder.1 = f32[4,2,32,128]{3,2,1,0:T(8,128)S(1)} custom-call(bf16[4,2,128,128]{3,2,1,0:T(8,128)(2,1)} %amps.1, bf16[1,1,64,128,128]{4,3,2,1,0:T(8,128)(2,1)} %factors.1, s32[2,4]{1,0:T(2,128)} %bitcast.2, s32[2,4]{1,0:T(2,128)} %bitcast.3), custom_call_target="tpu_custom_call" | custom-call | tf_op jit(solution)/shard_map/ladder/pallas_call | solution.py:315
  37.1 0.7 %copy.6 = f32[4,2,32,128]{3,2,1,0:T(8,128)} copy(f32[4,2,32,128]{3,2,1,0:T(8,128)S(1)} %ladder.1) | data formatting | bytes 262144

commit v4 on v3

--- a/solution.py
+++ b/solution.py
@@ -110,11 +110,14 @@
     rows = lax.broadcasted_iota(jnp.int32, (VIRT, VIRT), 0)
     cols = lax.broadcasted_iota(jnp.int32, (VIRT, VIRT), 1)
     reach = jnp.maximum(rows, cols)
-    for s in range(4):
-        for t in range(2):
-            g, p = s // 2, (s % 2) * 2 + t
-            tile = jnp.where(reach < counts[t, s], raw[s, t].astype(jnp.float32), 0.0)
-            masked[g, :, p * VIRT : (p + 1) * VIRT] = tile.astype(jnp.bfloat16)
+    def mask_group(g):
+        for sl in range(2):
+            for t in range(2):
+                s, p = 2 * g + sl, 2 * sl + t
+                tile = jnp.where(reach < counts[t, s], raw[s, t].astype(jnp.float32), 0.0)
+                masked[g, :, p * VIRT : (p + 1) * VIRT] = tile.astype(jnp.bfloat16)
+
+    mask_group(0)
 
     def part_copy(g, d):
         src = part.at[g, 1, 1 - core] if d == 1 else part.at[g, 0, core if d == 2 else 1 - core]
@@ -167,9 +170,8 @@
         flat = jnp.transpose(total)
         for vd in range(4):
             turned[g * 4 + vd] = flat[vd * SLAB : (vd + 1) * SLAB]
-        for h, vd, bx, dy in ROUTES:
-            if h == g and (bx or dy):
-                relay_copy(h, vd, bx, dy).start()
+            if any(route(g, vd)):
+                relay_copy(g, vd, *route(g, vd)).start()
         for h, vd, bx, dy in ROUTES:
             if h == g and not (bx or dy):
                 start_last_leg(h, vd, bx, dy)
@@ -247,6 +249,7 @@
 
     for copy in fac_copies:
         copy.wait()
+    mask_group(1)
     store_parts(0, 0, sum_products(0, far_row, 2 * SLAB, 0, AUX))
     send_parts(0)
     store_parts(1, 0, sum_products(1, far_row, 2 * SLAB, 0, AUX))

time: 37.9 us -> 37.8 us (level)
  no operation moved by 1% of the time
where the time goes in v4:
time: 37.8 us; the launch traced here: 37.7 us
  Pallas kernels  37 us (98%)
  local copies, waits for them, and re-layouts  0.66 us (2%)
    pallas_call x1, Pallas kernels, on_device(): pl.pallas_call(kernel, out_shape=jax.ShapeDtypeStruct((4, 2, SLAB, VIRT),...  37 us

profile of v4, /device:TPU:63, one launch (start us, length us, event | category | flops | bytes accessed | tf_op | source)
XLA Modules:
  0.0 37.7 jit_solution(15204052495210517545)
XLA Ops:
  0.0 37.0 %ladder.1 = f32[4,2,32,128]{3,2,1,0:T(8,128)S(1)} custom-call(bf16[4,2,128,128]{3,2,1,0:T(8,128)(2,1)} %amps.1, bf16[1,1,64,128,128]{4,3,2,1,0:T(8,128)(2,1)} %factors.1, s32[2,4]{1,0:T(2,128)} %bitcast.2, s32[2,4]{1,0:T(2,128)} %bitcast.3), custom_call_target="tpu_custom_call" | custom-call | tf_op jit(solution)/shard_map/ladder/pallas_call | solution.py:318
  37.0 0.7 %copy.6 = f32[4,2,32,128]{3,2,1,0:T(8,128)} copy(f32[4,2,32,128]{3,2,1,0:T(8,128)S(1)} %ladder.1) | data formatting | bytes 262144
